TPU v7x, 128 devices: a whole 4x4x4 slice. The times are simulated.
128 devices in a mesh: dp: 32 (over y, z_lo, x), mp: 4 (over z_hi, core).
Axes of the slice: x: 4, y: 4, z: 4 (z_hi: 2, z_lo: 2; z = z_hi * 2 + z_lo), core: 2. Of those that a mesh axis runs over, the one named last changes fastest.
Arguments:
- tokens: bfloat16 [64, 384, 1536], P('dp'), may hold values from -6 to 6
- cotangent: bfloat16 [64, 384, 1536], P('dp'), may hold values from -6 to 6
- lengths: int32 [64], replicated, may hold values from 96 to 384, as said below
- dealing: int32 [64], replicated, may hold values from 0 to 63, each once
- adapter_choice: int32 [64], replicated, may hold values from 0 to 7
- attention_gain: float32 [1536], replicated, may hold values from 0.5 to 1.5
- feedforward_gain: float32 [1536], replicated, may hold values from 0.5 to 1.5
- query_weight: bfloat16 [1536, 1536], P('dp', 'mp'), may hold values from -0.15625 to 0.15625
- key_weight: bfloat16 [1536, 768], P('dp', 'mp'), may hold values from -0.15625 to 0.15625
- value_weight: bfloat16 [1536, 768], P('dp', 'mp'), may hold values from -0.15625 to 0.15625
- output_weight: bfloat16 [1536, 1536], P('mp', 'dp'), may hold values from -0.4375 to 0.4375
- gate_weight: bfloat16 [1536, 4096], P('dp', 'mp'), may hold values from -0.15625 to 0.15625
- up_weight: bfloat16 [1536, 4096], P('dp', 'mp'), may hold values from -0.15625 to 0.15625
- down_weight: bfloat16 [4096, 1536], P('mp', 'dp'), may hold values from -0.09375 to 0.09375
- entry_qkv: bfloat16 [1536, 384], P('dp'), may hold values from -0.15625 to 0.15625
- exit_query: bfloat16 [128, 1536], P('dp', 'mp'), may hold values from -1.5 to 1.5
- exit_key: bfloat16 [128, 768], P('dp', 'mp'), may hold values from -1.5 to 1.5
- exit_value: bfloat16 [128, 768], P('dp', 'mp'), may hold values from -1.5 to 1.5
- entry_out: bfloat16 [1536, 128], P('mp', 'dp'), may hold values from -0.4375 to 0.4375
- exit_out: bfloat16 [128, 1536], P('dp'), may hold values from -1.5 to 1.5
- entry_gate_up: bfloat16 [1536, 256], P('dp'), may hold values from -0.15625 to 0.15625
- exit_gate: bfloat16 [128, 4096], P('dp', 'mp'), may hold values from -1.5 to 1.5
- exit_up: bfloat16 [128, 4096], P('dp', 'mp'), may hold values from -1.5 to 1.5
- entry_down: bfloat16 [4096, 128], P('mp', 'dp'), may hold values from -0.09375 to 0.09375
- exit_down: bfloat16 [128, 1536], P('dp'), may hold values from -1.5 to 1.5
Outputs:
- mixed: bfloat16 [64, 384, 1536], P('dp')
- input_grad: bfloat16 [64, 384, 1536], P('dp')
- grad_entry_qkv: float32 [1536, 384], P('dp')
- grad_exit_query: float32 [128, 1536], P('dp', 'mp')
- grad_exit_key: float32 [128, 768], P('dp', 'mp')
- grad_exit_value: float32 [128, 768], P('dp', 'mp')
- grad_entry_out: float32 [1536, 128], P('mp', 'dp')
- grad_exit_out: float32 [128, 1536], P('dp')
- grad_entry_gate_up: float32 [1536, 256], P('dp')
- grad_exit_gate: float32 [128, 4096], P('dp', 'mp')
- grad_exit_up: float32 [128, 4096], P('dp', 'mp')
- grad_entry_down: float32 [4096, 128], P('mp', 'dp')
- grad_exit_down: float32 [128, 1536], P('dp')
Inputs may be any that keep to these rules, and one draw needn't show every extreme that they name: `lengths`: each sequence has at least 96 tokens and some sequence exactly 384. `dealing`: each slot number appears once.
All inputs are finite; a program needn't handle non-finite values.
Results may differ from a plain program's by a relative error of at most 0.025.
Values may be sent and summed in bfloat16 or wider, within the bound.
No kernel may reach another device: no remote copies, remote signals or barrier semaphores. Data moves between devices by JAX's collectives and lax.ppermute only.
A program may use at most 192 MiB of HBM per device.

v0:
```python
import jax
import jax.numpy as jnp
from jax import lax
from jax.sharding import PartitionSpec as P

HEAD_DIM = 96
RANK = 16


EPS = 1e-05
THETA = 100000.0


def side_by_side(arrays, axis, dim, along):
    both = jnp.concatenate(arrays, axis=along)
    whole, at, outs = (lax.all_gather(both, axis, axis=dim, tiled=True), 0, [])
    for a in arrays:
        outs.append(lax.slice_in_dim(whole, at, at + a.shape[along], axis=along))
        at += a.shape[along]
    return tuple(outs)


def in_blocks(array, dim, devices):
    lengths = array.shape
    parts = array.reshape(*lengths[:dim], devices, lengths[dim] // devices, *lengths[dim + 1 :])
    return jnp.moveaxis(parts, dim, 0)


def one_scatter(arrays, axis, dims):
    devices = lax.axis_size(axis)
    parts = [in_blocks(a, dim, devices) for a, dim in zip(arrays, dims)]
    lines = jnp.concatenate([b.reshape(devices, -1) for b in parts], axis=1)
    extent = max(16, -(-lines.shape[1] // 1024) * 8)
    lines = jnp.pad(lines, ((0, 0), (0, extent * 128 - lines.shape[1]))).reshape(-1, 128)
    line, at, outs = (lax.psum_scatter(lines, axis, tiled=True).reshape(-1), 0, [])
    for b in parts:
        part = b[0]
        outs.append(line[at : at + part.size].reshape(part.shape))
        at += part.size
    return tuple(outs)


def matmul(left, right):
    return jnp.dot(left, right, preferred_element_type=jnp.float32)


def inner_rows(left, right):
    return lax.dot_general(
        left, right, (((0,), (0,)), ((), ())), preferred_element_type=jnp.float32
    )


def inner_cols(left, right):
    return lax.dot_general(
        left, right, (((1,), (1,)), ((), ())), preferred_element_type=jnp.float32
    )


def lookup(table, index):
    return jnp.sum(jnp.where(jnp.arange(table.shape[0]) == index, table, 0))


def rope_tables(count_rows):
    half = HEAD_DIM // 2
    freq = jnp.power(THETA, -2.0 * jnp.arange(half, dtype=jnp.float32) / HEAD_DIM)
    angle = jnp.arange(count_rows, dtype=jnp.float32)[:, None] * freq[None, :]
    return (jnp.cos(angle), jnp.sin(angle))


def rotate(values, cosine, sine):
    half = values.shape[-1] // 2
    first = values[..., :half]
    second = values[..., half:]
    cosine = cosine[:, None, :]
    sine = sine[:, None, :]
    return jnp.concatenate(
        [first * cosine - second * sine, second * cosine + first * sine], axis=-1
    )


def rms_scale(values):
    return lax.rsqrt(jnp.mean(values * values, axis=-1, keepdims=True) + EPS)


def norm_back(inputs, scale, gain, grad):
    weighted = gain * grad
    return scale * weighted - inputs * scale**3 * jnp.mean(
        inputs * weighted, axis=-1, keepdims=True
    )


def masked_scores(grouped, keys, allowed):
    raw = jnp.einsum("qjgd,kjd->jgqk", grouped, keys, preferred_element_type=jnp.float32)
    return jnp.where(allowed, raw * HEAD_DIM ** (-0.5), -1e30)


def forward(rows, length, chosen, attention_gain, feedforward_gain, weights):
    (
        query_weight,
        key_weight,
        value_weight,
        output_weight,
        gate_weight,
        up_weight,
        down_weight,
        entry_qkv,
        exit_query,
        exit_key,
        exit_value,
        entry_out,
        exit_out,
        entry_gate_up,
        exit_gate,
        exit_up,
        entry_down,
        exit_down,
    ) = weights
    count_rows = rows.shape[0]
    width = exit_query.shape[0]
    positions = jnp.arange(count_rows)
    live = positions < length
    select = (jnp.arange(width) // RANK == chosen).astype(jnp.float32)
    inputs = rows.astype(jnp.float32)
    scale_attn = rms_scale(inputs)
    normed = (inputs * scale_attn * attention_gain).astype(jnp.bfloat16)
    rank_qkv = (matmul(normed, entry_qkv) * jnp.tile(select, 3)).astype(jnp.bfloat16)
    queries = matmul(normed, query_weight) + matmul(rank_qkv[:, :width], exit_query)
    keys = matmul(normed, key_weight) + matmul(rank_qkv[:, width : 2 * width], exit_key)
    values = (matmul(normed, value_weight) + matmul(rank_qkv[:, 2 * width :], exit_value)).astype(
        jnp.bfloat16
    )
    cosine, sine = rope_tables(count_rows)
    queries = rotate(queries.reshape(count_rows, -1, HEAD_DIM), cosine, sine).astype(jnp.bfloat16)
    keys = rotate(keys.reshape(count_rows, -1, HEAD_DIM), cosine, sine).astype(jnp.bfloat16)
    kv_local = keys.shape[1]
    grouped = queries.reshape(count_rows, kv_local, -1, HEAD_DIM)
    allowed = (positions[None, :] <= positions[:, None]) & live[None, :]
    scores = masked_scores(grouped, keys, allowed)
    top = jnp.max(scores, axis=-1, keepdims=True)
    expd = jnp.exp(scores - top)
    total = jnp.sum(expd, axis=-1, keepdims=True)
    probs = expd / total
    log_total = top + jnp.log(total)
    attended = jnp.einsum(
        "jgqk,kjd->qjgd",
        probs.astype(jnp.bfloat16),
        values.reshape(count_rows, kv_local, HEAD_DIM),
        preferred_element_type=jnp.float32,
    )
    attended = attended.reshape(count_rows, -1).astype(jnp.bfloat16)
    projected, rank_part = lax.psum(
        (matmul(attended, output_weight), matmul(attended, entry_out)), "mp"
    )
    rank_out = (rank_part * select).astype(jnp.bfloat16)
    middle = inputs + projected + matmul(rank_out, exit_out)
    scale_mlp = rms_scale(middle)
    hidden_in = (middle * scale_mlp * feedforward_gain).astype(jnp.bfloat16)
    rank_gate_up = (matmul(hidden_in, entry_gate_up) * jnp.tile(select, 2)).astype(jnp.bfloat16)
    gate = matmul(hidden_in, gate_weight) + matmul(rank_gate_up[:, :width], exit_gate)
    up = matmul(hidden_in, up_weight) + matmul(rank_gate_up[:, width:], exit_up)
    activated = (jax.nn.silu(gate) * up).astype(jnp.bfloat16)
    reduced, rank_part_down = (
        lax.psum(matmul(activated, down_weight).astype(jnp.bfloat16), "mp").astype(jnp.float32),
        lax.psum(matmul(activated, entry_down).astype(jnp.bfloat16), "mp").astype(jnp.float32),
    )
    rank_down = (rank_part_down * select).astype(jnp.bfloat16)
    result = middle + reduced + matmul(rank_down, exit_down)
    mixed = jnp.where(live[:, None], result, 0.0).astype(jnp.bfloat16)
    saved = (
        inputs,
        scale_attn,
        normed,
        rank_qkv,
        queries,
        keys,
        values,
        log_total,
        attended,
        rank_out,
        middle,
        scale_mlp,
        hidden_in,
        rank_gate_up,
        gate,
        up,
        activated,
        rank_down,
        select,
        live,
        allowed,
        attention_gain,
        feedforward_gain,
    )
    return (mixed, saved)


def backward(cotangent_rows, weights, saved):
    (
        query_weight,
        key_weight,
        value_weight,
        output_weight,
        gate_weight,
        up_weight,
        down_weight,
        entry_qkv,
        exit_query,
        exit_key,
        exit_value,
        entry_out,
        exit_out,
        entry_gate_up,
        exit_gate,
        exit_up,
        entry_down,
        exit_down,
    ) = weights
    (
        inputs,
        scale_attn,
        normed,
        rank_qkv,
        queries,
        keys,
        values,
        log_total,
        attended,
        rank_out,
        middle,
        scale_mlp,
        hidden_in,
        rank_gate_up,
        gate,
        up,
        activated,
        rank_down,
        select,
        live,
        allowed,
        attention_gain,
        feedforward_gain,
    ) = saved
    width = exit_query.shape[0]
    count_rows = inputs.shape[0]
    grad_out = jnp.where(live[:, None], cotangent_rows.astype(jnp.float32), 0.0)
    rounded = grad_out.astype(jnp.bfloat16)
    grad_exit_down = inner_rows(rank_down, rounded)
    rank_grad = (inner_cols(rounded, exit_down) * select).astype(jnp.bfloat16)
    grad_entry_down = inner_rows(activated, rank_grad)
    grad_act = inner_cols(rounded, down_weight) + inner_cols(rank_grad, entry_down)
    sigma = jax.nn.sigmoid(gate)
    grad_up = (grad_act * gate * sigma).astype(jnp.bfloat16)
    grad_gate = (grad_act * up * sigma * (1.0 + gate * (1.0 - sigma))).astype(jnp.bfloat16)
    grad_exit_gate = inner_rows(rank_gate_up[:, :width], grad_gate)
    grad_exit_up = inner_rows(rank_gate_up[:, width:], grad_up)
    hidden_part = inner_cols(grad_gate, gate_weight) + inner_cols(grad_up, up_weight)
    rank_part = jnp.concatenate(
        [inner_cols(grad_gate, exit_gate), inner_cols(grad_up, exit_up)], axis=1
    )
    grad_hidden, rank_sum = lax.psum((hidden_part, rank_part), "mp")
    rank_grad = (rank_sum * jnp.tile(select, 2)).astype(jnp.bfloat16)
    grad_entry_gate_up = inner_rows(hidden_in, rank_grad)
    grad_hidden = grad_hidden + inner_cols(rank_grad, entry_gate_up)
    grad_middle = grad_out + norm_back(middle, scale_mlp, feedforward_gain, grad_hidden)
    rounded = grad_middle.astype(jnp.bfloat16)
    grad_exit_out = inner_rows(rank_out, rounded)
    rank_grad = (inner_cols(rounded, exit_out) * select).astype(jnp.bfloat16)
    grad_entry_out = inner_rows(attended, rank_grad)
    grad_attended = (inner_cols(rounded, output_weight) + inner_cols(rank_grad, entry_out)).astype(
        jnp.bfloat16
    )
    kv_local = keys.shape[1]
    grouped = queries.reshape(count_rows, kv_local, -1, HEAD_DIM)
    grad_grouped = grad_attended.reshape(count_rows, kv_local, -1, HEAD_DIM)
    scores = masked_scores(grouped, keys, allowed)
    probs = jnp.exp(scores - log_total)
    grad_probs = jnp.einsum(
        "qjgd,kjd->jgqk",
        grad_grouped,
        values.reshape(count_rows, kv_local, HEAD_DIM),
        preferred_element_type=jnp.float32,
    )
    delta = jnp.sum(probs * grad_probs, axis=-1, keepdims=True)
    grad_scores = (probs * (grad_probs - delta)).astype(jnp.bfloat16)
    factor = HEAD_DIM ** (-0.5)
    grad_rot_q = (
        jnp.einsum("jgqk,kjd->qjgd", grad_scores, keys, preferred_element_type=jnp.float32) * factor
    )
    grad_rot_k = (
        jnp.einsum("jgqk,qjgd->kjd", grad_scores, grouped, preferred_element_type=jnp.float32)
        * factor
    )
    grad_values = jnp.einsum(
        "jgqk,qjgd->kjd",
        probs.astype(jnp.bfloat16),
        grad_grouped,
        preferred_element_type=jnp.float32,
    )
    cosine, sine = rope_tables(count_rows)
    grad_queries = rotate(grad_rot_q.reshape(count_rows, -1, HEAD_DIM), cosine, -sine)
    grad_queries = grad_queries.reshape(count_rows, -1).astype(jnp.bfloat16)
    grad_keys = rotate(grad_rot_k, cosine, -sine).reshape(count_rows, -1).astype(jnp.bfloat16)
    grad_values = grad_values.reshape(count_rows, -1).astype(jnp.bfloat16)
    grad_exit_query = inner_rows(rank_qkv[:, :width], grad_queries)
    grad_exit_key = inner_rows(rank_qkv[:, width : 2 * width], grad_keys)
    grad_exit_value = inner_rows(rank_qkv[:, 2 * width :], grad_values)
    normed_part = (
        inner_cols(grad_queries, query_weight)
        + inner_cols(grad_keys, key_weight)
        + inner_cols(grad_values, value_weight)
    )
    rank_part = jnp.concatenate(
        [
            inner_cols(grad_queries, exit_query),
            inner_cols(grad_keys, exit_key),
            inner_cols(grad_values, exit_value),
        ],
        axis=1,
    )
    grad_normed, rank_sum = (
        lax.psum(normed_part.astype(jnp.bfloat16), "mp").astype(jnp.float32),
        lax.psum(rank_part.astype(jnp.bfloat16), "mp").astype(jnp.float32),
    )
    rank_grad = (rank_sum * jnp.tile(select, 3)).astype(jnp.bfloat16)
    grad_entry_qkv = inner_rows(normed, rank_grad)
    grad_normed = grad_normed + inner_cols(rank_grad, entry_qkv)
    grad_inputs = grad_middle + norm_back(inputs, scale_attn, attention_gain, grad_normed)
    terms = (
        grad_entry_qkv,
        grad_exit_query,
        grad_exit_key,
        grad_exit_value,
        grad_entry_out,
        grad_exit_out,
        grad_entry_gate_up,
        grad_exit_gate,
        grad_exit_up,
        grad_entry_down,
        grad_exit_down,
    )
    return (grad_inputs.astype(jnp.bfloat16), terms)


def per_device(
    tokens,
    cotangent,
    lengths,
    dealing,
    adapter_choice,
    attention_gain,
    feedforward_gain,
    query_weight,
    key_weight,
    value_weight,
    output_weight,
    gate_weight,
    up_weight,
    down_weight,
    entry_qkv,
    exit_query,
    exit_key,
    exit_value,
    entry_out,
    exit_out,
    entry_gate_up,
    exit_gate,
    exit_up,
    entry_down,
    exit_down,
):
    shards = (
        query_weight,
        key_weight,
        value_weight,
        output_weight,
        gate_weight,
        up_weight,
        down_weight,
        entry_qkv,
        exit_query,
        exit_key,
        exit_value,
        entry_out,
        exit_out,
        entry_gate_up,
        exit_gate,
        exit_up,
        entry_down,
        exit_down,
    )
    count = tokens.shape[0]
    first_slot = lax.axis_index("dp") * count
    outputs = []
    in_grads = []
    totals = None
    for micro in range(count):
        forward_weights = (
            *side_by_side((shards[0], shards[1], shards[2]), "dp", 0, 1),
            lax.all_gather(shards[3], "dp", axis=1, tiled=True),
            *side_by_side((shards[4], shards[5]), "dp", 0, 1),
            lax.all_gather(shards[6], "dp", axis=1, tiled=True),
            lax.all_gather(shards[7], "dp", axis=0, tiled=True),
            *side_by_side((shards[8], shards[9], shards[10]), "dp", 0, 1),
            lax.all_gather(shards[11], "dp", axis=1, tiled=True),
            lax.all_gather(shards[12], "dp", axis=0, tiled=True),
            lax.all_gather(shards[13], "dp", axis=0, tiled=True),
            *side_by_side((shards[14], shards[15]), "dp", 0, 1),
            lax.all_gather(shards[16], "dp", axis=1, tiled=True),
            lax.all_gather(shards[17], "dp", axis=0, tiled=True),
        )
        sequence = lookup(dealing, first_slot + micro)
        length = lookup(lengths, sequence)
        chosen = lookup(adapter_choice, sequence)
        mixed, saved = forward(
            tokens[micro], length, chosen, attention_gain, feedforward_gain, forward_weights
        )
        backward_weights = (
            *side_by_side((shards[0], shards[1], shards[2]), "dp", 0, 1),
            lax.all_gather(shards[3], "dp", axis=1, tiled=True),
            *side_by_side((shards[4], shards[5]), "dp", 0, 1),
            lax.all_gather(shards[6], "dp", axis=1, tiled=True),
            lax.all_gather(shards[7], "dp", axis=0, tiled=True),
            *side_by_side((shards[8], shards[9], shards[10]), "dp", 0, 1),
            lax.all_gather(shards[11], "dp", axis=1, tiled=True),
            lax.all_gather(shards[12], "dp", axis=0, tiled=True),
            lax.all_gather(shards[13], "dp", axis=0, tiled=True),
            *side_by_side((shards[14], shards[15]), "dp", 0, 1),
            lax.all_gather(shards[16], "dp", axis=1, tiled=True),
            lax.all_gather(shards[17], "dp", axis=0, tiled=True),
        )
        grad_rows, terms = backward(cotangent[micro], backward_weights, saved)
        outputs.append(mixed)
        in_grads.append(grad_rows)
        if micro == 0:
            totals = terms
        else:
            totals = jax.tree.map(jnp.add, totals, terms)
    shares = tuple(
        (
            part.astype(jnp.float32)
            for part in one_scatter(
                (
                    totals[0].astype(jnp.bfloat16),
                    totals[1].astype(jnp.bfloat16),
                    totals[2].astype(jnp.bfloat16),
                    totals[3].astype(jnp.bfloat16),
                    totals[4].astype(jnp.bfloat16),
                    totals[5].astype(jnp.bfloat16),
                    totals[6].astype(jnp.bfloat16),
                    totals[7].astype(jnp.bfloat16),
                    totals[8].astype(jnp.bfloat16),
                    totals[9].astype(jnp.bfloat16),
                    totals[10].astype(jnp.bfloat16),
                ),
                "dp",
                (0, 0, 0, 0, 1, 0, 0, 0, 0, 1, 0),
            )
        )
    )
    return (jnp.stack(outputs), jnp.stack(in_grads)) + tuple(shares)


def solution(mesh):
    return jax.shard_map(
        per_device,
        mesh=mesh,
        in_specs=(
            P("dp", None, None),
            P("dp", None, None),
            P(),
            P(),
            P(),
            P(),
            P(),
            P("dp", "mp"),
            P("dp", "mp"),
            P("dp", "mp"),
            P("mp", "dp"),
            P("dp", "mp"),
            P("dp", "mp"),
            P("mp", "dp"),
            P("dp", None),
            P("dp", "mp"),
            P("dp", "mp"),
            P("dp", "mp"),
            P("mp", "dp"),
            P("dp", None),
            P("dp", None),
            P("dp", "mp"),
            P("dp", "mp"),
            P("mp", "dp"),
            P("dp", None),
        ),
        out_specs=(
            P("dp", None, None),
            P("dp", None, None),
            P("dp", None),
            P("dp", "mp"),
            P("dp", "mp"),
            P("dp", "mp"),
            P("mp", "dp"),
            P("dp", None),
            P("dp", None),
            P("dp", "mp"),
            P("dp", "mp"),
            P("mp", "dp"),
            P("dp", None),
        ),
        check_vma=False,
    )
```

profile of v0, /device:TPU:0, one launch (start us, length us, event | category | flops | bytes accessed | tf_op | source)
XLA Modules:
  0.0 1571.9 jit_solution(10556218749791674027)
XLA Ops:
  17.0 83.1 %all-gather = bf16[32,4,768]{2,1,0:T(4,128)(2,1)S(1)} all-gather(bf16[1,4,768]{2,1,0:T(4,128)(2,1)S(1)} %maximum_bitcast_fusion.7), channel_id=1, replica_groups=mesh['dp'=32,'mp'=4] {'dp'}, dimensions={0}, use_global_device_ids=true | all-gather | bytes 202752 | tf_op jit(solution)/shard_map/all_gather | solution.py:16
  103.3 75.7 %all-gather.1 = bf16[32,4,384]{2,1,0:T(4,128)(2,1)S(1)} all-gather(bf16[1,4,384]{2,1,0:T(4,128)(2,1)S(1)} %bitcast.338), channel_id=1, replica_groups=mesh['dp'=32,'mp'=4] {'dp'}, dimensions={0}, use_global_device_ids=true | all-gather | bytes 101376 | tf_op jit(solution)/shard_map/all_gather | solution.py:404
  183.7 136.6 %all-gather.12.cloned.1.call-done = bf16[1536,768]{1,0:T(8,128)(2,1)} async-done(((bf16[48,768]{1,0:T(8,128)(2,1)}), bf16[1536,768]{1,0:T(8,128)(2,1)}) %all-gather.12.cloned.1.call-update) | async-done | bytes 2359312 | tf_op jit(solution)/shard_map/all_gather | solution.py:16
  335.3 138.1 %all-gather.16.cloned.1.call-done = bf16[384,1536]{0,1:T(8,128)(2,1)} async-done(((bf16[384,48]{0,1:T(8,128)(2,1)}), bf16[384,1536]{0,1:T(8,128)(2,1)}) %all-gather.16.cloned.1.call-update) | async-done | bytes 1179664 | tf_op jit(solution)/shard_map/all_gather | solution.py:399
  473.3 3.6 fusion.225
  476.9 2.7 fusion.223
  481.4 83.4 %all-gather.5 = bf16[32,4,1536]{2,1,0:T(4,128)(2,1)S(1)} all-gather(bf16[1,4,1536]{2,1,0:T(4,128)(2,1)S(1)} %bitcast.335), channel_id=1, replica_groups=mesh['dp'=32,'mp'=4] {'dp'}, dimensions={0}, use_global_device_ids=true | all-gather | bytes 405504 | tf_op jit(solution)/shard_map/all_gather | solution.py:409
  564.9 77.5 %all-gather.2 = bf16[32,4,1536]{2,1,0:T(4,128)(2,1)S(1)} all-gather(bf16[1,4,1536]{2,1,0:T(4,128)(2,1)S(1)} %bitcast.336), channel_id=1, replica_groups=mesh['dp'=32,'mp'=4] {'dp'}, dimensions={0}, use_global_device_ids=true | all-gather | bytes 405504 | tf_op jit(solution)/shard_map/all_gather | solution.py:405
  643.3 81.5 %all-gather.3 = bf16[32,4,2048]{2,1,0:T(4,128)(2,1)S(1)} all-gather(bf16[1,4,2048]{2,1,0:T(4,128)(2,1)S(1)} %maximum_bitcast_fusion.6), channel_id=1, replica_groups=mesh['dp'=32,'mp'=4] {'dp'}, dimensions={0}, use_global_device_ids=true | all-gather | bytes 540672 | tf_op jit(solution)/shard_map/all_gather | solution.py:16
  725.7 77.4 %all-gather.4 = bf16[32,4,1024]{2,1,0:T(4,128)(2,1)S(1)} all-gather(bf16[1,4,1024]{2,1,0:T(4,128)(2,1)S(1)} %bitcast.337), channel_id=1, replica_groups=mesh['dp'=32,'mp'=4] {'dp'}, dimensions={0}, use_global_device_ids=true | all-gather | bytes 270336 | tf_op jit(solution)/shard_map/all_gather | solution.py:408
  805.0 2.4 fusion.97
  808.6 89.2 %all_gather.31 = bf16[1536,256]{1,0:T(8,128)(2,1)} all-gather(bf16[48,256]{1,0:T(8,128)(2,1)S(1)} %copy-done.124), channel_id=1, replica_groups=mesh['dp'=32,'mp'=4] {'dp'}, dimensions={0}, use_global_device_ids=true | all-gather | bytes 811008 | tf_op jit(solution)/shard_map/all_gather | solution.py:406
  897.8 5.0 fusion.209
  902.8 2.7 fusion.205
  905.5 2.9 multiply_reduce_fusion.3
  914.7 3.8 fusion.54
  938.6 2.9 convolution_add_fusion.13
  941.5 2.8 convolution_add_fusion.14
  945.8 2.2 convolution_convert_fusion.6
  948.0 2.2 convolution_convert_fusion.7
  950.2 5.0 convolution_convert_fusion
  955.2 2.5 convolution_convert_fusion.1
  957.7 98.2 %all-reduce.12.cloned.1.call-done = (f32[384,1536]{1,0:T(8,128)}, f32[384,256]{1,0:T(8,128)}, f32[384,1536]{1,0:T(8,128)}, f32[384,256]{1,0:T(8,128)}) async-done(((f32[384,1536]{1,0:T(8,128)}, f32[384,256]{1,0:T(8,128)}, f32[384,1536]{1,0:T(8,128)}, f32[384,256]{1,0:T(8,128)}), (f32[384,1536]{1,0:T(8,128)}, f32[384,256]{1,0:T(8,128)}, f32[384,1536]{1,0:T(8,128)}, ...) | async-done | bytes 5505040 | tf_op jit(solution)/shard_map/psum | solution.py:260
  1056.0 2.7 multiply_reduce_fusion.1
  1097.6 2.3 copy.107
  1112.8 2.2 fusion.14
  1120.7 78.5 %all-reduce.16.cloned.1.call-done = (bf16[384,1536]{1,0:T(8,128)(2,1)}, bf16[384,128]{1,0:T(8,128)(2,1)}, bf16[384,1536]{1,0:T(8,128)(2,1)}, bf16[384,128]{1,0:T...) async-done(((bf16[384,1536]{1,0:T(8,128)(2,1)}, bf16[384,128]{1,0:T(8,128)(2,1)}, ...) | async-done | bytes 5505040 | tf_op jit(solution)/shard_map/psum | solution.py:163
  1199.3 2.5 fusion.125
  1223.1 4.3 pad.4
  1227.3 5.5 reshape.369
  1234.9 2.3 fusion
  1247.5 305.2 %all-reduce.10.cloned.1.call-done = bf16[15104,128]{1,0:T(8,128)(2,1)} async-done(((bf16[15104,128]{1,0:T(8,128)(2,1)}), bf16[15104,128]{1,0:T(8,128)(2,1)}) %all-reduce.10.cloned.1.call-update) | async-done | bytes 3866640
  (585 shorter events, 167.7 us)
Async XLA Ops:
  7.2 173.3 %copy-start.13 = (bf16[2,384,1536]{2,1,0:T(8,128)(2,1)S(1)}, bf16[2,384,1536]{2,1,0:T(8,128)(2,1)}, u32[]{:S(2)}) copy-start(bf16[2,384,1536]{2,1,0:T(8,128)(2,1)} %param.25) | copy-start | bytes 7077892
  7.3 96.1 %copy-start.174 = (bf16[384,4]{0,1:T(4,128)(2,1)S(1)}, bf16[384,4]{0,1:T(4,128)(2,1)}, u32[]{:S(2)}) copy-start(bf16[384,4]{0,1:T(4,128)(2,1)} %param.43) | copy-start | bytes 9220
  7.3 173.3 %copy-start.119 = (f32[1536]{0:T(1024)S(1)}, f32[1536]{0:T(1024)}, u32[]{:S(2)}) copy-start(f32[1536]{0:T(1024)} %param.30) | copy-start | bytes 18436
  7.3 173.2 %all-gather.14.cloned.1.call-start = ((), (), s32[]{:S(2)}) async-start(), calls=%async_computation.1 | async-start | bytes 1216512 | tf_op jit(solution)/shard_map/all_gather | solution.py:402
  8.0 312.2 %all-gather.12.cloned.1.call-start = ((), (), s32[]{:S(2)}) async-start(), calls=%async_computation | async-start | bytes 2433024 | tf_op jit(solution)/shard_map/all_gather | solution.py:16
  9.6 463.7 %all-gather.16.cloned.1.call-start = ((), (), s32[]{:S(2)}) async-start(), calls=%async_computation.2 | async-start | bytes 1216512 | tf_op jit(solution)/shard_map/all_gather | solution.py:399
  10.3 887.4 %all-gather.20.cloned.1.call-start = ((), (), s32[]{:S(2)}) async-start(), calls=%async_computation.4 | async-start | bytes 3244032 | tf_op jit(solution)/shard_map/all_gather | solution.py:401
  10.9 894.5 %all-reduce.14.cloned.1.call-start = ((), (), s32[]{:S(2)}) async-start(), calls=%async_computation.7 | async-start | bytes 10223616 | tf_op jit(solution)/shard_map/psum | solution.py:151
  16.9 165.8 %copy-start.141 = (f32[384]{0:T(512)}, f32[384]{0:T(512)S(1)}, u32[]{:S(2)}) copy-start(f32[384]{0:T(512)S(1)} %broadcast_bitcast_fusion) | copy-start | bytes 4612
  100.2 233.2 %copy-start.25 = (bf16[128,768]{1,0:T(8,128)(2,1)}, bf16[128,768]{1,0:T(8,128)(2,1)S(1)}, u32[]{:S(2)}) copy-start(bf16[128,768]{1,0:T(8,128)(2,1)S(1)} %reshape.386) | copy-start | bytes 589828
  100.9 81.9 %copy-start.143 = (f32[384]{0:T(512)}, f32[384]{0:T(512)S(1)}, u32[]{:S(2)}) copy-start(f32[384]{0:T(512)S(1)} %broadcast_bitcast_fusion.1) | copy-start | bytes 4612
  101.9 224.1 %copy-start.61 = (f32[384,48]{0,1:T(8,128)}, f32[384,48]{0,1:T(8,128)S(1)}, u32[]{:S(2)}) copy-start(f32[384,48]{0,1:T(8,128)S(1)} %get-tuple-element.120) | copy-start | bytes 221188
  179.1 155.2 %copy-start.48 = (bf16[128,384]{1,0:T(8,128)(2,1)}, bf16[128,384]{1,0:T(8,128)(2,1)S(1)}, u32[]{:S(2)}) copy-start(bf16[128,384]{1,0:T(8,128)(2,1)S(1)} %reshape.388) | copy-start | bytes 294916
  180.5 144.2 %copy-start.147 = (f32[384]{0:T(512)}, f32[384]{0:T(512)S(1)}, u32[]{:S(2)}) copy-start(f32[384]{0:T(512)S(1)} %get-tuple-element.113) | copy-start | bytes 4612
  182.8 146.9 %copy-start.71 = (bf16[384,384]{1,0:T(8,128)(2,1)}, bf16[384,384]{1,0:T(8,128)(2,1)S(1)}, u32[]{:S(2)}) copy-start(bf16[384,384]{1,0:T(8,128)(2,1)S(1)} %fusion.63) | copy-start | bytes 884740
  183.6 149.7 %copy-start.70 = (bf16[384,384]{1,0:T(8,128)(2,1)}, bf16[384,384]{1,0:T(8,128)(2,1)S(1)}, u32[]{:S(2)}) copy-start(bf16[384,384]{1,0:T(8,128)(2,1)S(1)} %fusion.62) | copy-start | bytes 884740
  333.7 139.7 %copy-start.46 = (bf16[2,96,2,384]{3,1,2,0:T(8,128)(2,1)S(1)}, bf16[2,96,2,384]{3,1,2,0:T(8,128)(2,1)}, u32[]{:S(2)}) copy-start(bf16[2,96,2,384]{3,1,2,0:T(8,128)(2,1)} %copy-done.45) | copy-start | bytes 884740
  334.3 145.4 %copy-start.43 = (bf16[2,96,2,384]{3,1,2,0:T(8,128)(2,1)}, bf16[2,96,2,384]{3,1,2,0:T(8,128)(2,1)S(1)}, u32[]{:S(2)}) copy-start(bf16[2,96,2,384]{3,1,2,0:T(8,128)(2,1)S(1)} %convolution_convert_fusion.3) | copy-start | bytes 884740
  479.7 85.2 %copy-start.138 = (bf16[4,1536]{1,0:T(4,128)(2,1)S(1)}, bf16[4,1536]{1,0:T(4,128)(2,1)}, u32[]{:S(2)}) copy-start(bf16[4,1536]{1,0:T(4,128)(2,1)} %param.44) | copy-start | bytes 36868
  479.7 163.6 %copy-start.157 = (bf16[4,1024]{1,0:T(4,128)(2,1)S(1)}, bf16[4,1024]{1,0:T(4,128)(2,1)}, u32[]{:S(2)}) copy-start(bf16[4,1024]{1,0:T(4,128)(2,1)} %param.47) | copy-start | bytes 24580
  479.7 163.6 %copy-start.158 = (bf16[4,1024]{1,0:T(4,128)(2,1)S(1)}, bf16[4,1024]{1,0:T(4,128)(2,1)}, u32[]{:S(2)}) copy-start(bf16[4,1024]{1,0:T(4,128)(2,1)} %param.46) | copy-start | bytes 24580
  479.7 246.0 %copy-start.156 = (bf16[1024,4]{0,1:T(4,128)(2,1)S(1)}, bf16[1024,4]{0,1:T(4,128)(2,1)}, u32[]{:S(2)}) copy-start(bf16[1024,4]{0,1:T(4,128)(2,1)} %param.48) | copy-start | bytes 24580
  479.8 435.0 %all-gather.18.cloned.1.call-start = ((), (), s32[]{:S(2)}) async-start(), calls=%async_computation.3 | async-start | bytes 6488064 | tf_op jit(solution)/shard_map/all_gather | solution.py:16
  481.3 574.6 %all-reduce.12.cloned.1.call-start = ((), (), s32[]{:S(2)}) async-start(), calls=%async_computation.6 | async-start | bytes 11010048 | tf_op jit(solution)/shard_map/psum | solution.py:260
  481.4 322.5 %copy-start.134 = (f32[128]{0:T(128)S(1)}, f32[128]{0:T(128)}, u32[]{:S(2)}) copy-start(f32[128]{0:T(128)} %copy-done.133) | copy-start | bytes 1540
  481.4 323.1 %copy-start.130 = (f32[128]{0:T(128)S(1)}, f32[128]{0:T(128)}, u32[]{:S(2)}) copy-start(f32[128]{0:T(128)} %copy-done.129) | copy-start | bytes 1540
  481.4 323.6 %copy-start.160 = (pred[384]{0:T(512)(128)(4,1)S(1)}, pred[384]{0:T(512)(128)(4,1)}, u32[]{:S(2)}) copy-start(pred[384]{0:T(512)(128)(4,1)} %copy-done.159) | copy-start | bytes 1156
  564.9 242.5 %copy-start.35 = (bf16[128,1536]{1,0:T(8,128)(2,1)}, bf16[128,1536]{1,0:T(8,128)(2,1)S(1)}, u32[]{:S(2)}) copy-start(bf16[128,1536]{1,0:T(8,128)(2,1)S(1)} %reshape.396) | copy-start | bytes 1179652
  724.8 82.6 %copy-start.165 = (pred[384]{0:T(512)(128)(4,1)S(1)}, pred[384]{0:T(512)(128)(4,1)}, u32[]{:S(2)}) copy-start(pred[384]{0:T(512)(128)(4,1)} %copy-done.164) | copy-start | bytes 1156
  908.4 147.6 %copy-start.3 = (f32[384,1536]{1,0:T(8,128)}, f32[384,1536]{1,0:T(8,128)S(1)}, u32[]{:S(2)}) copy-start(f32[384,1536]{1,0:T(8,128)S(1)} %get-tuple-element.126) | copy-start | bytes 7077892
  944.3 254.9 %all-reduce.16.cloned.1.call-start = ((), (), s32[]{:S(2)}) async-start(), calls=%async_computation.8 | async-start | bytes 11010048 | tf_op jit(solution)/shard_map/psum | solution.py:163
  1084.4 468.4 %all-reduce.10.cloned.1.call-start = ((), (), s32[]{:S(2)}) async-start(), calls=%async_computation.5 | async-start | bytes 7733248
  (163 other events, 919.0 us)
Sparse Core Ops, SparseCore 0:
  9.8 154.0 all-gather.13
  166.1 154.0 all-gather.11
  321.9 151.4 all-gather.15
  474.8 155.7 all-gather.19
  633.8 112.8 all-reduce.13
  748.3 163.1 all-gather.17
  944.4 111.4 all-reduce.11
  1084.5 114.7 all-reduce.15
  1233.0 319.6 all-reduce.9
where the time goes:
time: 1580 us; the launch traced here: 1570 us
  waiting for transfers between devices  759 us (48%)
  blocking collectives  568 us (36%)
  matrix products  126 us (8%)
  local copies, waits for them, and re-layouts  70.4 us (4%)
  other arithmetic  31.4 us (2%)
  between operations  17.1 us (1%)
    unnamed x10, waiting for transfers between devices  307 us
    all_gather x2, blocking collectives, side_by_side(): whole, at, outs = (lax.all_gather(both, axis, axis=dim, tiled=True), 0, [])  165 us
    all_gather x1, waiting for transfers between devices, per_device(): lax.all_gather(shards[3], 'dp', axis=1, tiled=True)  138 us
    all_gather x2, waiting for transfers between devices, side_by_side(): whole, at, outs = (lax.all_gather(both, axis, axis=dim, tiled=True), 0, [])  137 us
    psum x1, waiting for transfers between devices, backward(): grad_hidden, rank_sum = lax.psum((hidden_part, rank_part), 'mp')  98.2 us
    all_gather x1, blocking collectives, per_device(): lax.all_gather(shards[13], 'dp', axis=0, tiled=True)  89.2 us
    all_gather x1, blocking collectives, per_device(): lax.all_gather(shards[17], 'dp', axis=0, tiled=True)  83.4 us
    psum x1, waiting for transfers between devices, forward(): lax.psum(matmul(activated, down_weight).astype(jnp.bfloat16), 'mp')  78.5 us
  transfers between devices with their start and end apart: 9, of which 5 were waited for; matrix products, arithmetic and copies ran while one was open for 7% of the time, Pallas kernels for 0%

commit v1 on v0

v1 whole, which is shorter than its diff:
```python
import jax
import jax.numpy as jnp
from jax import lax
from jax.experimental import pallas as pl
from jax.experimental.pallas import tpu as pltpu
from jax.sharding import Mesh, PartitionSpec as P

HEAD_DIM = 96
RANK = 16
EPS = 1e-05
THETA = 100000.0
BF = jnp.bfloat16
F32 = jnp.float32

AXES = ("y", "zl", "x", "zh", "c")
SIZES = (4, 2, 4, 2, 2)
ORDERS = ("xyz", "yzx", "zxy")
ATTN, GATE_UP, DOWN = 2048, 2048, 1024
WIDTHS = (ATTN, GATE_UP, DOWN)


def device_index(y, z, x, c):
    return (((y * 2 + z % 2) * 4 + x) * 2 + z // 2) * 2 + c


def flip_pairs(axis, flips):
    pairs = []
    for y in range(4):
        for z in range(4):
            for x in range(4):
                for c in range(2):
                    at = {"x": x, "y": y, "z": z}
                    to = dict(at)
                    to[axis] ^= flips[c]
                    pairs.append(
                        (device_index(y, z, x, c), device_index(to["y"], to["z"], to["x"], c))
                    )
    return pairs


def core_swap(value):
    pairs = [(i, i ^ 1) for i in range(128)]
    return lax.ppermute(value, AXES, pairs)


class Links:
    def __init__(self, depth):
        self.depth = depth
        self.sent = {axis: [] for axis in depth}

    def __call__(self, value, axis, flips):
        sent, depth = self.sent[axis], self.depth[axis]
        if len(sent) >= depth:
            value, _ = lax.optimization_barrier((value, sent[-depth]))
        out = lax.ppermute(value, AXES, flip_pairs(axis, flips))
        sent.append(out)
        return out


def ring_stage(send, blocks, stage, forward):
    axes = [order[stage] for order in ORDERS]
    near = [send(b, a, (1, 3)) for b, a in zip(blocks, axes)]
    far = [send(b, a, (3, 1)) for b, a in zip(blocks, axes)]
    if not forward:
        across = [send(b, a, (2, 2)) for b, a in zip(blocks, axes)]
        return [[b, n, o, f] for b, n, o, f in zip(blocks, near, across, far)]
    half = blocks[0].shape[0] // 2
    low = [send(n[:half], a, (3, 1)) for n, a in zip(near, axes)]
    high = [send(f[half:], a, (1, 3)) for f, a in zip(far, axes)]
    return [[b, n, lo, hi, f] for b, n, lo, hi, f in zip(blocks, near, low, high, far)]


def place_kernel(widths, coords, *refs):
    pieces, outs, sem = refs[:15], refs[15 : 15 + len(widths)], refs[-1]
    own = {"y": coords[0], "z": coords[1], "x": coords[2]}
    core = coords[3]

    def relative(j):
        return j if j % 2 == 0 else jnp.where(core == 0, j, 4 - j)

    at = {axis: [own[axis] ^ relative(j) for j in range(4)] for axis in "xyz"}
    row = {
        "y": [v * 384 for v in at["y"]],
        "z": [lax.rem(v, 2) * 192 for v in at["z"]],
        "x": [v * 48 for v in at["x"]],
    }
    high = [lax.div(v, 2) for v in at["z"]]
    for part, order in enumerate(ORDERS):
        for q, (j3, k0, count) in enumerate(
            ((0, 0, 16), (1, 0, 16), (2, 0, 8), (2, 8, 8), (3, 0, 16))
        ):
            piece = pieces[part * 5 + q]
            for k in range(count):
                j = {order[2]: j3, order[1]: (k0 + k) // 4, order[0]: (k0 + k) % 4}
                first = row["y"][j["y"]] + row["z"][j["z"]] + row["x"][j["x"]] + part * 16
                first = pl.multiple_of(first, 16)
                start = 0
                for g, width in enumerate(widths):
                    pltpu.make_async_copy(
                        piece.at[k, :, pl.ds(start, width)],
                        outs[g].at[high[j["z"]], pl.ds(first, 16), :],
                        sem.at[g],
                    ).start()
                    start += width
    for g in range(len(widths)):
        pltpu.make_async_copy(outs[g], outs[g], sem.at[g]).wait()


def place(pieces, coords, widths):
    return pl.pallas_call(
        lambda *refs: place_kernel(widths, *refs),
        out_shape=[jax.ShapeDtypeStruct((2, 1536, w), BF) for w in widths],
        in_specs=[pl.BlockSpec(memory_space=pltpu.SMEM)]
        + [pl.BlockSpec(memory_space=pl.ANY)] * len(pieces),
        out_specs=[pl.BlockSpec(memory_space=pl.ANY)] * len(widths),
        scratch_shapes=[pltpu.SemaphoreType.DMA((len(widths),))],
    )(coords, *pieces)


def matmul(left, right):
    return jnp.dot(left, right, preferred_element_type=F32)


def inner_rows(left, right):
    return lax.dot_general(left, right, (((0,), (0,)), ((), ())), preferred_element_type=F32)


def inner_cols(left, right):
    return lax.dot_general(left, right, (((1,), (1,)), ((), ())), preferred_element_type=F32)


def lookup(table, index):
    return jnp.sum(jnp.where(jnp.arange(table.shape[0]) == index, table, 0))


def rope_tables(count_rows):
    half = HEAD_DIM // 2
    freq = jnp.power(THETA, -2.0 * jnp.arange(half, dtype=F32) / HEAD_DIM)
    angle = jnp.arange(count_rows, dtype=F32)[:, None] * freq[None, :]
    return (jnp.cos(angle), jnp.sin(angle))


def rotate(values, cosine, sine):
    half = values.shape[-1] // 2
    first = values[..., :half]
    second = values[..., half:]
    cosine = cosine[:, None, :]
    sine = sine[:, None, :]
    return jnp.concatenate(
        [first * cosine - second * sine, second * cosine + first * sine], axis=-1
    )


def rms_scale(values):
    return lax.rsqrt(jnp.mean(values * values, axis=-1, keepdims=True) + EPS)


def norm_back(inputs, scale, gain, grad):
    weighted = gain * grad
    return scale * weighted - inputs * scale**3 * jnp.mean(
        inputs * weighted, axis=-1, keepdims=True
    )


def both(parts):
    widths = [p.shape[1] for p in parts]
    sent = jnp.concatenate([p.astype(BF) for p in parts], axis=1)
    got, at, outs = core_swap(sent), 0, []
    for p, w in zip(parts, widths):
        outs.append(p + got[:, at : at + w].astype(F32))
        at += w
    return outs


def per_device(
    tokens,
    cotangent,
    lengths,
    dealing,
    adapter_choice,
    attention_gain,
    feedforward_gain,
    query_weight,
    key_weight,
    value_weight,
    output_weight,
    gate_weight,
    up_weight,
    down_weight,
    entry_qkv,
    exit_query,
    exit_key,
    exit_value,
    entry_out,
    exit_out,
    entry_gate_up,
    exit_gate,
    exit_up,
    entry_down,
    exit_down,
):
    y, zl, x, zh, core = (lax.axis_index(a) for a in AXES)
    own_high = zh == 0
    entries = jnp.concatenate([entry_qkv, entry_gate_up], axis=1)
    entries = jnp.where(own_high, entries[:, :320], entries[:, 320:])
    exits = jnp.concatenate(
        [
            exit_query,
            exit_key,
            exit_value,
            exit_gate,
            exit_up,
            entry_out.T,
            entry_down.T,
            jnp.where(own_high, exit_out, exit_down),
            jnp.zeros((4, 384), BF),
        ],
        axis=1,
    ).reshape(48, 512)
    payload = jnp.concatenate(
        [
            query_weight,
            key_weight,
            value_weight,
            output_weight.T,
            entries,
            jnp.zeros((48, 64), BF),
            exits,
            gate_weight,
            up_weight,
            down_weight.T,
        ],
        axis=1,
    )
    send = Links({"x": 2, "y": 1, "z": 2})
    blocks = [payload[None, 16 * i : 16 * i + 16] for i in range(3)]
    blocks = [jnp.concatenate(p, 0) for p in ring_stage(send, blocks, 0, False)]
    blocks = [jnp.concatenate(p, 0) for p in ring_stage(send, blocks, 1, True)]
    pieces = sum(ring_stage(send, blocks, 2, True), [])
    coords = jnp.stack([y, zh * 2 + zl, x, core]).astype(jnp.int32)
    attn_w, gate_up_w, down_w = place(pieces, coords, WIDTHS)

    slot = ((y * 2 + zl) * 4 + x) * 2 + zh
    sequence = lookup(dealing, slot)
    length = lookup(lengths, sequence)
    chosen = lookup(adapter_choice, sequence)
    rows = lax.dynamic_index_in_dim(tokens, zh, 0, keepdims=False)
    cot = lax.dynamic_index_in_dim(cotangent, zh, 0, keepdims=False)
    count = rows.shape[0]

    def own16(wide, parts):
        return jnp.concatenate(
            [
                lax.dynamic_slice_in_dim(wide[:, i * 128 : i * 128 + 128], chosen * RANK, RANK, 1)
                for i in range(parts)
            ],
            axis=1,
        )

    qkv_w = [attn_w[h, :, :768] for h in range(2)]
    out_w = [attn_w[h, :, 768:1152] for h in range(2)]
    gate_w = [gate_up_w[h, :, :1024] for h in range(2)]
    up_w = [gate_up_w[h, :, 1024:] for h in range(2)]
    entry = jnp.concatenate([attn_w[0, :, 1152:1472], attn_w[1, :, 1152:1472]], axis=1)
    entry_a = own16(entry, 5)
    ent_qkv, ent_gu = entry_a[:, :48], entry_a[:, 48:]
    mine = lax.dynamic_slice(attn_w, (0, chosen * 192, 1536), (2, 192, 512)).reshape(2, RANK, 6144)
    x_q = [mine[h, :, :384] for h in range(2)]
    x_k = [mine[h, :, 384:576] for h in range(2)]
    x_v = [mine[h, :, 576:768] for h in range(2)]
    x_gate = [mine[h, :, 768:1792] for h in range(2)]
    x_up = [mine[h, :, 1792:2816] for h in range(2)]
    e_out = [mine[h, :, 2816:3200] for h in range(2)]
    e_down = [mine[h, :, 3200:4224] for h in range(2)]
    x_out, x_down = mine[0, :, 4224:5760], mine[1, :, 4224:5760]

    positions = jnp.arange(count)
    live = positions < length
    allowed = (positions[None, :] <= positions[:, None]) & live[None, :]
    inputs = rows.astype(F32)
    scale_attn = rms_scale(inputs)
    normed = (inputs * scale_attn * attention_gain).astype(BF)
    rank_qkv = matmul(normed, ent_qkv).astype(BF)
    r_q, r_k, r_v = rank_qkv[:, :16], rank_qkv[:, 16:32], rank_qkv[:, 32:]
    q_parts, k_parts, v_parts = [], [], []
    for h in range(2):
        qkv = matmul(normed, qkv_w[h])
        q_parts.append(qkv[:, :384] + matmul(r_q, x_q[h]))
        k_parts.append(qkv[:, 384:576] + matmul(r_k, x_k[h]))
        v_parts.append(qkv[:, 576:] + matmul(r_v, x_v[h]))
    cosine, sine = rope_tables(count)

    def heads(parts):
        return jnp.concatenate(parts, axis=1).reshape(count, -1, HEAD_DIM)

    queries = rotate(heads(q_parts), cosine, sine).astype(BF)
    keys = rotate(heads(k_parts), cosine, sine).astype(BF)
    values = heads(v_parts).astype(BF)
    kv = keys.shape[1]
    grouped = queries.reshape(count, kv, -1, HEAD_DIM)
    factor = HEAD_DIM ** (-0.5)
    raw = jnp.einsum("qjgd,kjd->jgqk", grouped, keys, preferred_element_type=F32)
    scores = jnp.where(allowed, raw * factor, -1e30)
    top = jnp.max(scores, axis=-1, keepdims=True)
    expd = jnp.exp(scores - top)
    probs = expd / jnp.sum(expd, axis=-1, keepdims=True)
    probs16 = probs.astype(BF)
    attended = jnp.einsum("jgqk,kjd->qjgd", probs16, values, preferred_element_type=F32)
    attended = attended.reshape(count, -1).astype(BF)
    att = [attended[:, :384], attended[:, 384:]]
    projected, rank_part = both(
        [
            inner_cols(att[0], out_w[0]) + inner_cols(att[1], out_w[1]),
            inner_cols(att[0], e_out[0]) + inner_cols(att[1], e_out[1]),
        ]
    )
    rank_out = rank_part.astype(BF)
    middle = inputs + projected + matmul(rank_out, x_out)
    scale_mlp = rms_scale(middle)
    hidden_in = (middle * scale_mlp * feedforward_gain).astype(BF)
    rank_gu = matmul(hidden_in, ent_gu).astype(BF)
    r_gate, r_up = rank_gu[:, :16], rank_gu[:, 16:]

    grad_out = jnp.where(live[:, None], cot.astype(F32), 0.0)
    g2 = grad_out.astype(BF)
    drank_down = inner_cols(g2, x_down).astype(BF)
    act, g_gate, g_up = [], [], []
    for h in range(2):
        gate = matmul(hidden_in, gate_w[h]) + matmul(r_gate, x_gate[h])
        up = matmul(hidden_in, up_w[h]) + matmul(r_up, x_up[h])
        sigma = jax.nn.sigmoid(gate)
        act.append((gate * sigma * up).astype(BF))
        grad_act = matmul(g2, down_w[h]) + matmul(drank_down, e_down[h])
        g_up.append((grad_act * gate * sigma).astype(BF))
        g_gate.append((grad_act * up * sigma * (1.0 + gate * (1.0 - sigma))).astype(BF))
    reduced, rank_part = both(
        [
            inner_cols(act[0], down_w[0]) + inner_cols(act[1], down_w[1]),
            inner_cols(act[0], e_down[0]) + inner_cols(act[1], e_down[1]),
        ]
    )
    rank_down = rank_part.astype(BF)
    result = middle + reduced + matmul(rank_down, x_down)
    mixed = jnp.where(live[:, None], result, 0.0).astype(BF)

    grad_hidden, drank_gate, drank_up = both(
        [
            sum(inner_cols(g_gate[h], gate_w[h]) + inner_cols(g_up[h], up_w[h]) for h in range(2)),
            sum(inner_cols(g_gate[h], x_gate[h]) for h in range(2)),
            sum(inner_cols(g_up[h], x_up[h]) for h in range(2)),
        ]
    )
    drank_gu = jnp.concatenate([drank_gate, drank_up], axis=1).astype(BF)
    grad_hidden = grad_hidden + inner_cols(drank_gu, ent_gu)
    grad_middle = grad_out + norm_back(middle, scale_mlp, feedforward_gain, grad_hidden)
    g1 = grad_middle.astype(BF)
    drank_out = inner_cols(g1, x_out).astype(BF)
    grad_att = [(matmul(g1, out_w[h]) + matmul(drank_out, e_out[h])).astype(BF) for h in range(2)]
    g_grouped = jnp.concatenate(grad_att, axis=1).reshape(count, kv, -1, HEAD_DIM)
    grad_probs = jnp.einsum("qjgd,kjd->jgqk", g_grouped, values, preferred_element_type=F32)
    delta = jnp.sum(probs * grad_probs, axis=-1, keepdims=True)
    grad_scores = (probs * (grad_probs - delta)).astype(BF)
    g_rq = jnp.einsum("jgqk,kjd->qjgd", grad_scores, keys, preferred_element_type=F32) * factor
    g_rk = jnp.einsum("jgqk,qjgd->kjd", grad_scores, grouped, preferred_element_type=F32) * factor
    g_v = jnp.einsum("jgqk,qjgd->kjd", probs16, g_grouped, preferred_element_type=F32)
    g_q = rotate(g_rq.reshape(count, -1, HEAD_DIM), cosine, -sine).reshape(count, -1).astype(BF)
    g_k = rotate(g_rk, cosine, -sine).reshape(count, -1).astype(BF)
    g_v = g_v.reshape(count, -1).astype(BF)
    gq = [g_q[:, :384], g_q[:, 384:]]
    gk = [g_k[:, :192], g_k[:, 192:]]
    gv = [g_v[:, :192], g_v[:, 192:]]
    gqkv = [jnp.concatenate([gq[h], gk[h], gv[h]], axis=1) for h in range(2)]
    grad_normed, d_q, d_k, d_v = both(
        [
            inner_cols(gqkv[0], qkv_w[0]) + inner_cols(gqkv[1], qkv_w[1]),
            inner_cols(gq[0], x_q[0]) + inner_cols(gq[1], x_q[1]),
            inner_cols(gk[0], x_k[0]) + inner_cols(gk[1], x_k[1]),
            inner_cols(gv[0], x_v[0]) + inner_cols(gv[1], x_v[1]),
        ]
    )
    drank_qkv = jnp.concatenate([d_q, d_k, d_v], axis=1).astype(BF)
    grad_normed = grad_normed + inner_cols(drank_qkv, ent_qkv)
    grad_in = grad_middle + norm_back(inputs, scale_attn, attention_gain, grad_normed)
    grad_in = grad_in.astype(BF)

    columns = jnp.stack(
        [
            jnp.concatenate(
                [
                    inner_rows(r_q, gq[h]),
                    inner_rows(r_k, gk[h]),
                    inner_rows(r_v, gv[h]),
                    inner_rows(r_gate, g_gate[h]),
                    inner_rows(r_up, g_up[h]),
                    inner_rows(drank_out, att[h]),
                    inner_rows(drank_down, act[h]),
                ],
                axis=1,
            )
            for h in range(2)
        ]
    ).astype(BF)
    shared = jnp.concatenate([inner_rows(rank_out, g1), inner_rows(rank_down, g2)], axis=1)
    shared = shared.astype(BF)
    wide = jnp.concatenate(
        [
            inner_rows(normed, drank_qkv),
            inner_rows(hidden_in, drank_gu),
            jnp.zeros((1536, 48), F32),
        ],
        axis=1,
    ).astype(BF)
    lines = jnp.concatenate(
        [
            columns.reshape(2, 4, 132, 128),
            jnp.broadcast_to(shared.reshape(1, 4, 96, 128), (2, 4, 96, 128)),
            jnp.broadcast_to(
                wide.reshape(8, 4, 48, 128).transpose(1, 0, 2, 3).reshape(1, 4, 384, 128),
                (2, 4, 384, 128),
            ),
        ],
        axis=2,
    ).reshape(8, 612, 128)
    got = lax.all_to_all(lines, ("zh", "x"), 0, 0, tiled=True)
    peers = ((y * 2 + zl) * 4 + jnp.tile(jnp.arange(4), 2)) * 2 + jnp.repeat(jnp.arange(2), 4)
    match = (jnp.arange(64)[None, :] == peers[:, None]).astype(jnp.int32)
    peer_seq = jnp.sum(match * dealing[None, :], axis=1)
    match = (jnp.arange(64)[None, :] == peer_seq[:, None]).astype(jnp.int32)
    peer_adapter = jnp.sum(match * adapter_choice[None, :], axis=1)
    one_hot = (jnp.arange(8)[:, None] == peer_adapter[None, :]).astype(BF)
    summed = jnp.einsum("as,slk->alk", one_hot, got, preferred_element_type=F32).astype(BF)
    second = jnp.concatenate(
        [
            summed[:, :228],
            summed[:, 228:].reshape(8, 8, 48, 128).transpose(1, 0, 2, 3).reshape(8, 384, 128),
        ],
        axis=1,
    )
    final = lax.all_to_all(second, ("y", "zl"), 0, 0, tiled=True)
    final = jnp.sum(final.astype(F32), axis=0)
    cols = final[:132].reshape(4, 4224)
    shared = final[132:228].reshape(4, 3072)
    wide = final[228:].reshape(8, 48, 128).transpose(1, 2, 0)
    wide_qkv = wide[:, :48].reshape(48, 3, 16, 8).transpose(0, 1, 3, 2).reshape(48, 384)
    wide_gu = wide[:, 48:80].reshape(48, 2, 16, 8).transpose(0, 1, 3, 2).reshape(48, 256)

    def share(value):
        other = lax.ppermute(value, AXES, flip_pairs("z", (2, 2)))
        return jnp.stack([jnp.where(own_high, value, other), jnp.where(own_high, other, value)])

    return (
        share(mixed),
        share(grad_in),
        wide_qkv,
        cols[:, :384],
        cols[:, 384:576],
        cols[:, 576:768],
        cols[:, 2816:3200].T,
        shared[:, :1536],
        wide_gu,
        cols[:, 768:1792],
        cols[:, 1792:2816],
        cols[:, 3200:].T,
        shared[:, 1536:],
    )


def solution(mesh):
    fine = Mesh(mesh.devices.reshape(SIZES), AXES)
    dp, mp = ("y", "zl", "x"), ("zh", "c")
    return jax.shard_map(
        per_device,
        mesh=fine,
        in_specs=(
            P(dp, None, None),
            P(dp, None, None),
            P(),
            P(),
            P(),
            P(),
            P(),
            P(dp, mp),
            P(dp, mp),
            P(dp, mp),
            P(mp, dp),
            P(dp, mp),
            P(dp, mp),
            P(mp, dp),
            P(dp, None),
            P(dp, mp),
            P(dp, mp),
            P(dp, mp),
            P(mp, dp),
            P(dp, None),
            P(dp, None),
            P(dp, mp),
            P(dp, mp),
            P(mp, dp),
            P(dp, None),
        ),
        out_specs=(
            P(dp, None, None),
            P(dp, None, None),
            P(dp, None),
            P(dp, mp),
            P(dp, mp),
            P(dp, mp),
            P(mp, dp),
            P(dp, None),
            P(dp, None),
            P(dp, mp),
            P(dp, mp),
            P(mp, dp),
            P(dp, None),
        ),
        check_vma=False,
    )
```

time: 1580 us -> 1440 us (0.911)
  Pallas kernels: 0 us -> 955 us
  waiting for transfers between devices: 759 us -> 164 us
  blocking collectives: 568 us -> 0 us
  starting transfers between devices: 0.77 us -> 63.9 us
    pallas_call x0 -> x1, Pallas kernels: none -> 955 us  [place(): pl.pallas_call(lambda *refs: place_kernel(widths, *refs), out_shape=[jax....]
    all_gather x7 -> x0, blocking collectives: 568 us -> none  [the longest x2 165 us: side_by_side(): whole, at, outs = (lax.all_gather(both, axis, axis=dim, tiled=True), 0, [])]
    unnamed x10 -> x0, waiting for transfers between devices: 307 us -> none
    all_gather x5 -> x0, waiting for transfers between devices: 275 us -> none  [the longest x1 138 us: per_device(): lax.all_gather(shards[3], 'dp', axis=1, tiled=True)]
    psum x3 -> x0, waiting for transfers between devices: 177 us -> none  [the longest x1 98.2 us: backward(): grad_hidden, rank_sum = lax.psum((hidden_part, rank_part), 'mp')]
    ppermute x0 -> x39, waiting for transfers between devices: none -> 151 us  [the longest x33 126 us: __call__(): out = lax.ppermute(value, AXES, flip_pairs(axis, flips))]
    ppermute x0 -> x39, starting transfers between devices: none -> 56.3 us  [the longest x33 49.1 us: __call__(): out = lax.ppermute(value, AXES, flip_pairs(axis, flips))]
    unnamed x391 -> x235, local copies, waits for them, and re-layouts: 36.3 us -> 13.2 us
  transfers between devices with their start and end apart: 9 -> 41, of which waited for: 5 -> 18; matrix products, arithmetic and copies ran while one was open for 7% -> 10% of each run, Pallas kernels for 0% -> 0%
where the time goes in v1:
time: 1440 us; the launch traced here: 1430 us
  Pallas kernels  955 us (66%)
  waiting for transfers between devices  164 us (11%)
  matrix products  134 us (9%)
  local copies, waits for them, and re-layouts  75.7 us (5%)
  starting transfers between devices  63.9 us (4%)
  other arithmetic  35.6 us (2%)
    pallas_call x1, Pallas kernels, place(): pl.pallas_call(lambda *refs: place_kernel(widths, *refs), out_shape=[jax....  955 us
    ppermute x33, waiting for transfers between devices, __call__(): out = lax.ppermute(value, AXES, flip_pairs(axis, flips))  126 us
    dot_general x28, matrix products, inner_cols(): lax.dot_general(left, right, (((1,), (1,)), ((), ())), preferred_element_...  59.6 us
    ppermute x33, starting transfers between devices, __call__(): out = lax.ppermute(value, AXES, flip_pairs(axis, flips))  49.1 us
    dot_general x28, matrix products, matmul(): return jnp.dot(left, right, preferred_element_type=F32)  44 us
  transfers between devices with their start and end apart: 41, of which 18 were waited for; matrix products, arithmetic and copies ran while one was open for 10% of the time, Pallas kernels for 0%

profile of v1, /device:TPU:0, one launch (start us, length us, event | category | flops | bytes accessed | tf_op | source)
XLA Modules:
  0.0 1432.1 jit_solution(2872510805103293265)
XLA Ops:
  25.2 3.3 collective-permute-start.5
  28.7 3.4 collective-permute-done.5
  42.7 4.3 collective-permute-start.7
  55.6 3.2 collective-permute-start.8
  58.9 8.2 collective-permute-done.8
  67.2 7.0 collective-permute-done.9
  75.6 34.2 %collective-permute-done.29.refs_12_ = bf16[16,16,5120]{2,1,0:T(8,128)(2,1)S(1)} collective-permute-done((bf16[16,16,5120]{2,1,0:T(8,128)(2,1)S(1)}, bf16[16,16,5120]{2,1,0:T(8,128)(2,1)S(1)}, u32[]{:S(2)}, u32[]{:S(2)}) %collective-permute-start.29) | collective-permute-done | bytes 2621472 | tf_op jit(solution)/shard_map/ppermute | solution.py:55
  109.8 3.4 collective-permute-start.30
  113.9 28.9 %collective-permute-done.30.refs_15_ = bf16[16,16,5120]{2,1,0:T(8,128)(2,1)S(1)} collective-permute-done((bf16[16,16,5120]{2,1,0:T(8,128)(2,1)S(1)}, bf16[16,16,5120]{2,1,0:T(8,128)(2,1)S(1)}, u32[]{:S(2)}, u32[]{:S(2)}) %collective-permute-start.30) | collective-permute-done | bytes 2621472 | tf_op jit(solution)/shard_map/ppermute | solution.py:55
  142.8 3.2 collective-permute-start.31
  150.4 20.8 %collective-permute-done.19.refs_5_ = bf16[16,16,5120]{2,1,0:T(8,128)(2,1)S(1)} collective-permute-done((bf16[16,16,5120]{2,1,0:T(8,128)(2,1)S(1)}, bf16[16,16,5120]{2,1,0:T(8,128)(2,1)S(1)}, u32[]{:S(2)}, u32[]{:S(2)}) %collective-permute-start.19) | collective-permute-done | bytes 2621472 | tf_op jit(solution)/shard_map/ppermute | solution.py:55
  185.7 4.8 collective-permute-done.20.refs_4_
  195.8 954.7 %shard_map.336 = (bf16[2,1536,2048]{2,1,0:T(8,128)(2,1)}, bf16[2,1536,2048]{2,1,0:T(8,128)(2,1)}, bf16[2,1536,1024]{2,1,0:T(8,128)(2,1)}) custom-call(s32[4]{0:T(128)} %pad_add_fusion.refs_0_, bf16[16,16,5120]{2,1,0:T(8,128)(2,1)} %copy-done.26, bf16[16,16,5120]{2,1,0:T(8,128)(2,1)} %copy-done.14, bf16[8,16,5120]{2,1,0:T(8,128)(2,1)} %collective-permute-done.14.refs_3_, ...), custom_call_target="tpu_custom_call" | custom-call | tf_op jit(solution)/shard_map/pallas_call | solution.py:110
  1152.4 3.8 fusion.78
  1156.2 3.8 fusion.75
  1173.0 4.0 fusion.263
  1182.6 3.5 fusion.265
  1193.4 4.8 fusion.93
  1209.0 3.4 fusion.90
  1233.1 4.4 fusion.38
  1237.5 5.3 fusion.268
  1242.9 3.3 concatenate.153
  1249.1 5.0 fusion.7
  1255.9 5.7 fusion.267
  1275.5 3.5 select_convert_fusion
  1365.8 4.0 all-to-all-start
  1370.3 3.6 collective-permute-start.38
  1373.9 3.2 select_bitcast_fusion.3
  1377.1 12.9 all-to-all-done
  1392.1 3.6 all-to-all-start.1
  1395.7 3.2 pad_maximum_fusion
  1399.0 25.2 %collective-permute-done.38 = bf16[384,1536]{1,0:T(8,128)(2,1)} collective-permute-done((bf16[384,1536]{1,0:T(8,128)(2,1)S(1)}, bf16[384,1536]{1,0:T(8,128)(2,1)}, u32[]{:S(2)}, u32[]{:S(2)}) %collective-permute-start.38) | collective-permute-done | bytes 1179680 | tf_op jit(solution)/shard_map/ppermute | solution.py:448
  (507 shorter events, 242.2 us)
Async XLA Ops:
  6.5 14.5 %collective-permute-start.10 = (bf16[1,16,5120]{2,1,0:T(8,128)(2,1)S(1)}, bf16[1,16,5120]{2,1,0:T(8,128)(2,1)S(1)}, u32[]{:S(2)}, u32[]{:S(2)}) collective-permute-start(bf16[1,16,5120]{2,1,0:T(8,128)(2,1)S(1)} %get-tuple-element.55), channel_id=1, source_target_pairs={{0,18},{1,17},{4,22},{5,21},{8,26},{9,25},{12,30},{13,29},{16,2},{... | collective-permute-start | bytes 491528 | tf_op jit(solution)/shard_map/ppermute | solution.py:55
  9.0 12.7 collective-permute-start.2
  21.8 17.5 %collective-permute-start.21 = (bf16[4,16,5120]{2,1,0:T(8,128)(2,1)S(1)}, bf16[4,16,5120]{2,1,0:T(8,128)(2,1)S(1)}, u32[]{:S(2)}, u32[]{:S(2)}) collective-permute-start(bf16[4,16,5120]{2,1,0:T(8,128)(2,1)S(1)} %pad_maximum_fusion.9), channel_id=1, source_target_pairs={{0,4},{1,13},{4,0},{5,9},{8,12},{9,5},{12,8},{13,1},{16,20},{17,29... | collective-permute-start | bytes 1966088 | tf_op jit(solution)/shard_map/ppermute | solution.py:55
  23.9 16.9 %collective-permute-start.25 = (bf16[4,16,5120]{2,1,0:T(8,128)(2,1)S(1)}, bf16[4,16,5120]{2,1,0:T(8,128)(2,1)S(1)}, u32[]{:S(2)}, u32[]{:S(2)}) collective-permute-start(bf16[4,16,5120]{2,1,0:T(8,128)(2,1)S(1)} %pad_maximum_fusion.9), channel_id=1, source_target_pairs={{0,12},{1,5},{4,8},{5,1},{8,4},{9,13},{12,0},{13,9},{16,28},{17,21... | collective-permute-start | bytes 1966088 | tf_op jit(solution)/shard_map/ppermute | solution.py:55
  32.1 10.6 collective-permute-start.6
  33.9 15.3 %collective-permute-start.11 = (bf16[4,16,5120]{2,1,0:T(8,128)(2,1)S(1)}, bf16[4,16,5120]{2,1,0:T(8,128)(2,1)S(1)}, u32[]{:S(2)}, u32[]{:S(2)}) collective-permute-start(bf16[4,16,5120]{2,1,0:T(8,128)(2,1)S(1)} %pad_maximum_fusion.8), channel_id=1, source_target_pairs={{0,16},{1,19},{4,20},{5,23},{8,24},{9,27},{12,28},{13,31},{16,0},{... | collective-permute-start | bytes 1966088 | tf_op jit(solution)/shard_map/ppermute | solution.py:55
  35.6 16.4 %collective-permute-start.17 = (bf16[4,16,5120]{2,1,0:T(8,128)(2,1)S(1)}, bf16[4,16,5120]{2,1,0:T(8,128)(2,1)S(1)}, u32[]{:S(2)}, u32[]{:S(2)}) collective-permute-start(bf16[4,16,5120]{2,1,0:T(8,128)(2,1)S(1)} %pad_maximum_fusion.8), channel_id=1, source_target_pairs={{0,18},{1,17},{4,22},{5,21},{8,26},{9,25},{12,30},{13,29},{16,2},{... | collective-permute-start | bytes 1966088 | tf_op jit(solution)/shard_map/ppermute | solution.py:55
  39.3 14.3 collective-permute-start.22
  40.9 17.9 %collective-permute-start.26 = (bf16[2,16,5120]{2,1,0:T(8,128)(2,1)S(1)}, bf16[2,16,5120]{2,1,0:T(8,128)(2,1)S(1)}, u32[]{:S(2)}, u32[]{:S(2)}) collective-permute-start(bf16[2,16,5120]{2,1,0:T(8,128)(2,1)S(1)} %slice.433), channel_id=1, source_target_pairs={{0,4},{1,13},{4,0},{5,9},{8,12},{9,5},{12,8},{13,1},{16,20},{17,29... | collective-permute-start | bytes 983048 | tf_op jit(solution)/shard_map/ppermute | solution.py:55
  42.7 12.9 collective-permute-start.7
  49.3 25.0 %collective-permute-start.12 = (bf16[2,16,5120]{2,1,0:T(8,128)(2,1)S(1)}, bf16[2,16,5120]{2,1,0:T(8,128)(2,1)S(1)}, u32[]{:S(2)}, u32[]{:S(2)}) collective-permute-start(bf16[2,16,5120]{2,1,0:T(8,128)(2,1)S(1)} %slice.427), channel_id=1, source_target_pairs={{0,18},{1,17},{4,22},{5,21},{8,26},{9,25},{12,30},{13,29},{16,2},{... | collective-permute-start | bytes 983048 | tf_op jit(solution)/shard_map/ppermute | solution.py:55
  52.1 22.2 %collective-permute-start.18 = (bf16[2,16,5120]{2,1,0:T(8,128)(2,1)S(1)}, bf16[2,16,5120]{2,1,0:T(8,128)(2,1)S(1)}, u32[]{:S(2)}, u32[]{:S(2)}) collective-permute-start(bf16[2,16,5120]{2,1,0:T(8,128)(2,1)S(1)} %slice.429), channel_id=1, source_target_pairs={{0,16},{1,19},{4,20},{5,23},{8,24},{9,27},{12,28},{13,31},{16,0},{... | collective-permute-start | bytes 983048 | tf_op jit(solution)/shard_map/ppermute | solution.py:55
  55.6 11.5 collective-permute-start.8
  74.2 35.6 %collective-permute-start.29 = (bf16[16,16,5120]{2,1,0:T(8,128)(2,1)S(1)}, bf16[16,16,5120]{2,1,0:T(8,128)(2,1)S(1)}, u32[]{:S(2)}, u32[]{:S(2)}) collective-permute-start(bf16[16,16,5120]{2,1,0:T(8,128)(2,1)S(1)} %constant_dynamic-update-slice_fusion.16.refs_11_), channel_id=1, source_target_pairs={{0,32},{1,97},{4,36},{5,101},{8,40},{9,105},{12,44},{13,109},{16,4... | collective-permute-start | bytes 7864328 | tf_op jit(solution)/shard_map/ppermute | solution.py:55
  74.4 71.6 %collective-permute-start.27 = (bf16[16,16,5120]{2,1,0:T(8,128)(2,1)S(1)}, bf16[16,16,5120]{2,1,0:T(8,128)(2,1)S(1)}, u32[]{:S(2)}, u32[]{:S(2)}) collective-permute-start(bf16[16,16,5120]{2,1,0:T(8,128)(2,1)S(1)} %constant_dynamic-update-slice_fusion.8.refs_6_), channel_id=1, source_target_pairs={{0,12},{1,5},{4,8},{5,1},{8,4},{9,13},{12,0},{13,9},{16,28},{17,21... | collective-permute-start | bytes 7864328 | tf_op jit(solution)/shard_map/ppermute | solution.py:55
  75.6 71.8 %collective-permute-start.23 = (bf16[16,16,5120]{2,1,0:T(8,128)(2,1)S(1)}, bf16[16,16,5120]{2,1,0:T(8,128)(2,1)S(1)}, u32[]{:S(2)}, u32[]{:S(2)}) collective-permute-start(bf16[16,16,5120]{2,1,0:T(8,128)(2,1)S(1)} %constant_dynamic-update-slice_fusion.8.refs_6_), channel_id=1, source_target_pairs={{0,4},{1,13},{4,0},{5,9},{8,12},{9,5},{12,8},{13,1},{16,20},{17,29... | collective-permute-start | bytes 7864328 | tf_op jit(solution)/shard_map/ppermute | solution.py:55
  109.8 33.1 %collective-permute-start.30 = (bf16[16,16,5120]{2,1,0:T(8,128)(2,1)S(1)}, bf16[16,16,5120]{2,1,0:T(8,128)(2,1)S(1)}, u32[]{:S(2)}, u32[]{:S(2)}) collective-permute-start(bf16[16,16,5120]{2,1,0:T(8,128)(2,1)S(1)} %constant_dynamic-update-slice_fusion.16.refs_11_), channel_id=1, source_target_pairs={{0,96},{1,33},{4,100},{5,37},{8,104},{9,41},{12,108},{13,45},{16,1... | collective-permute-start | bytes 7864328 | tf_op jit(solution)/shard_map/ppermute | solution.py:55
  113.3 57.8 %collective-permute-start.19 = (bf16[16,16,5120]{2,1,0:T(8,128)(2,1)S(1)}, bf16[16,16,5120]{2,1,0:T(8,128)(2,1)S(1)}, u32[]{:S(2)}, u32[]{:S(2)}) collective-permute-start(bf16[16,16,5120]{2,1,0:T(8,128)(2,1)S(1)} %constant_dynamic-update-slice_fusion.refs_1_), channel_id=1, source_target_pairs={{0,18},{1,17},{4,22},{5,21},{8,26},{9,25},{12,30},{13,29},{16,2},{... | collective-permute-start | bytes 7864328 | tf_op jit(solution)/shard_map/ppermute | solution.py:55
  113.4 59.1 %collective-permute-start.13 = (bf16[16,16,5120]{2,1,0:T(8,128)(2,1)S(1)}, bf16[16,16,5120]{2,1,0:T(8,128)(2,1)S(1)}, u32[]{:S(2)}, u32[]{:S(2)}) collective-permute-start(bf16[16,16,5120]{2,1,0:T(8,128)(2,1)S(1)} %constant_dynamic-update-slice_fusion.refs_1_), channel_id=1, source_target_pairs={{0,16},{1,19},{4,20},{5,23},{8,24},{9,27},{12,28},{13,31},{16,0},{... | collective-permute-start | bytes 7864328 | tf_op jit(solution)/shard_map/ppermute | solution.py:55
  142.8 33.5 %collective-permute-start.31 = (bf16[8,16,5120]{2,1,0:T(8,128)(2,1)S(1)}, bf16[8,16,5120]{2,1,0:T(8,128)(2,1)S(1)}, u32[]{:S(2)}, u32[]{:S(2)}) collective-permute-start(bf16[8,16,5120]{2,1,0:T(8,128)(2,1)S(1)} %slice.435), channel_id=1, source_target_pairs={{0,96},{1,33},{4,100},{5,37},{8,104},{9,41},{12,108},{13,45},{16,1... | collective-permute-start | bytes 3932168 | tf_op jit(solution)/shard_map/ppermute | solution.py:55
  147.3 38.3 %collective-permute-start.28 = (bf16[8,16,5120]{2,1,0:T(8,128)(2,1)}, bf16[8,16,5120]{2,1,0:T(8,128)(2,1)}, u32[]{:S(2)}, u32[]{:S(2)}) collective-permute-start(bf16[8,16,5120]{2,1,0:T(8,128)(2,1)} %slice.434), channel_id=1, source_target_pairs={{0,4},{1,13},{4,0},{5,9},{8,12},{9,5},{12,8},{13,1},{16,20},{17,29... | collective-permute-start | bytes 3932168 | tf_op jit(solution)/shard_map/ppermute | solution.py:55
  148.6 37.1 %collective-permute-start.24 = (bf16[8,16,5120]{2,1,0:T(8,128)(2,1)}, bf16[8,16,5120]{2,1,0:T(8,128)(2,1)}, u32[]{:S(2)}, u32[]{:S(2)}) collective-permute-start(bf16[8,16,5120]{2,1,0:T(8,128)(2,1)} %slice.432), channel_id=1, source_target_pairs={{0,12},{1,5},{4,8},{5,1},{8,4},{9,13},{12,0},{13,9},{16,28},{17,21... | collective-permute-start | bytes 3932168 | tf_op jit(solution)/shard_map/ppermute | solution.py:55
  172.4 18.0 %collective-permute-start.20 = (bf16[8,16,5120]{2,1,0:T(8,128)(2,1)}, bf16[8,16,5120]{2,1,0:T(8,128)(2,1)}, u32[]{:S(2)}, u32[]{:S(2)}) collective-permute-start(bf16[8,16,5120]{2,1,0:T(8,128)(2,1)} %slice.430), channel_id=1, source_target_pairs={{0,16},{1,19},{4,20},{5,23},{8,24},{9,27},{12,28},{13,31},{16,0},{... | collective-permute-start | bytes 3932168 | tf_op jit(solution)/shard_map/ppermute | solution.py:55
  173.7 19.1 %collective-permute-start.14 = (bf16[8,16,5120]{2,1,0:T(8,128)(2,1)}, bf16[8,16,5120]{2,1,0:T(8,128)(2,1)}, u32[]{:S(2)}, u32[]{:S(2)}) collective-permute-start(bf16[8,16,5120]{2,1,0:T(8,128)(2,1)} %slice.428), channel_id=1, source_target_pairs={{0,18},{1,17},{4,22},{5,21},{8,26},{9,25},{12,30},{13,29},{16,2},{... | collective-permute-start | bytes 3932168 | tf_op jit(solution)/shard_map/ppermute | solution.py:55
  177.4 18.4 %collective-permute-start.32 = (bf16[8,16,5120]{2,1,0:T(8,128)(2,1)}, bf16[8,16,5120]{2,1,0:T(8,128)(2,1)}, u32[]{:S(2)}, u32[]{:S(2)}) collective-permute-start(bf16[8,16,5120]{2,1,0:T(8,128)(2,1)} %slice.436), channel_id=1, source_target_pairs={{0,32},{1,97},{4,36},{5,101},{8,40},{9,105},{12,44},{13,109},{16,4... | collective-permute-start | bytes 3932168 | tf_op jit(solution)/shard_map/ppermute | solution.py:55
  1188.7 12.1 collective-permute-start.33
  1248.6 34.8 %collective-permute-start.36 = (bf16[384,1568]{0,1:T(8,128)(2,1)}, bf16[384,1568]{0,1:T(8,128)(2,1)}, u32[]{:S(2)}, u32[]{:S(2)}) collective-permute-start(bf16[384,1568]{0,1:T(8,128)(2,1)} %copy.318), channel_id=1, source_target_pairs={{0,1},{1,0},{2,3},{3,2},{4,5},{5,4},{6,7},{7,6},{8,9},{9,8},{10,11... | collective-permute-start | bytes 3612680 | tf_op jit(solution)/shard_map/ppermute | solution.py:43
  1279.0 94.9 %collective-permute-start.35 = (bf16[384,1536]{1,0:T(8,128)(2,1)}, bf16[384,1536]{1,0:T(8,128)(2,1)}, u32[]{:S(2)}, u32[]{:S(2)}) collective-permute-start(bf16[384,1536]{1,0:T(8,128)(2,1)} %select_convert_fusion), channel_id=1, source_target_pairs={{0,2},{1,3},{4,6},{5,7},{8,10},{9,11},{12,14},{13,15},{16,18},{17,... | collective-permute-start | bytes 3538952 | tf_op jit(solution)/shard_map/ppermute | solution.py:448
  1334.2 17.2 %collective-permute-start.37 = (bf16[384,1584]{0,1:T(8,128)(2,1)}, bf16[384,1584]{0,1:T(8,128)(2,1)}, u32[]{:S(2)}, u32[]{:S(2)}) collective-permute-start(bf16[384,1584]{0,1:T(8,128)(2,1)} %copy.326), channel_id=1, source_target_pairs={{0,1},{1,0},{2,3},{3,2},{4,5},{5,4},{6,7},{7,6},{8,9},{9,8},{10,11... | collective-permute-start | bytes 3649544 | tf_op jit(solution)/shard_map/ppermute | solution.py:43
  1365.8 24.3 %all-to-all-start = ((bf16[8,612,128]{2,1,0:T(8,128)(2,1)}), bf16[8,612,128]{2,1,0:T(8,128)(2,1)S(1)}, u32[]{:S(2)}, u32[]{:S(2)}) async-start(bf16[8,612,128]{2,1,0:T(8,128)(2,1)} %pad_maximum_fusion.4), calls=%async_computation | async-start | bytes 2523136 | tf_op jit(solution)/shard_map/all_to_all | solution.py:424
  1370.3 53.8 %collective-permute-start.38 = (bf16[384,1536]{1,0:T(8,128)(2,1)S(1)}, bf16[384,1536]{1,0:T(8,128)(2,1)}, u32[]{:S(2)}, u32[]{:S(2)}) collective-permute-start(bf16[384,1536]{1,0:T(8,128)(2,1)S(1)} %copy-done.17), channel_id=1, source_target_pairs={{0,2},{1,3},{4,6},{5,7},{8,10},{9,11},{12,14},{13,15},{16,18},{17,... | collective-permute-start | bytes 3538952 | tf_op jit(solution)/shard_map/ppermute | solution.py:448
  1392.1 35.0 %all-to-all-start.1 = ((bf16[8,612,128]{2,1,0:T(8,128)(2,1)}), bf16[8,612,128]{2,1,0:T(8,128)(2,1)S(1)}, u32[]{:S(2)}, u32[]{:S(2)}) async-start(bf16[8,612,128]{2,1,0:T(8,128)(2,1)} %pad_maximum_fusion.5), calls=%async_computation.1 | async-start | bytes 2523136 | tf_op jit(solution)/shard_map/all_to_all | solution.py:439
  (114 other events, 3690.1 us)
